TPU v7x, 32 devices: a whole 2x2x4 slice. The times are simulated.
32 devices in a mesh: query: 2 (over x), corpus: 16 (over z, y, core).
Axes of the slice: x: 2, y: 2, z: 4, core: 2. Of those that a mesh axis runs over, the one named last changes fastest.
Arguments:
- clean_feats: bfloat16 [2, 2, 512, 320], P('query', None, 'corpus'), may hold values from -6 to 6
- noise_draw: bfloat16 [2, 2, 512, 320], P('query', None, 'corpus'), may hold values from -6 to 6
- timesteps: int32 [2, 2], P('query'), may hold values from 0 to 999
- weight_in: bfloat16 [2, 320, 320], P(None, None, 'corpus'), may hold values from -0.3125 to 0.3125
- weight_ffin: bfloat16 [2, 320, 2560], P(None, None, 'corpus'), may hold values from -0.3125 to 0.3125
- weight_ffout: bfloat16 [2, 1280, 320], P(None, None, 'corpus'), may hold values from -0.15625 to 0.15625
- weight_out: bfloat16 [2, 320, 320], P(None, None, 'corpus'), may hold values from -0.3125 to 0.3125
- norm_gain: float32 [2, 320], replicated, may hold values from 0.5 to 1.5
- norm_bias: float32 [2, 320], replicated, may hold values from -3 to 3
- sketch_cin: bfloat16 [2, 3, 320, 16], replicated, may hold values from -0.3125 to 0.3125
- sketch_fin: bfloat16 [2, 1280, 16], replicated, may hold values from -0.15625 to 0.15625
- sketch_cout: bfloat16 [2, 3, 320, 16], replicated, may hold values from -0.3125 to 0.3125
- sketch_fout: bfloat16 [2, 2560, 16], replicated, may hold values from -0.125 to 0.125
- precond: float32 [8, 256, 256], P('query'), as said below
- store_grads: bfloat16 [8192, 2048], P(('query', 'corpus')), may hold values from -6 to 6
- store_scale: float32 [8192], P(('query', 'corpus')), may hold values from 0.002 to 0.03
Outputs:
- scores: float32 [2, 8192], P(None, ('query', 'corpus'))
Inputs may be any that keep to these rules, and one draw needn't show every extreme that they name: `precond`: each layer's matrix is symmetric with a diagonal between 1 and 2.
All inputs are finite; a program needn't handle non-finite values.
Results may differ from a plain program's by a relative error of at most 0.0085.
Values may be sent and summed in bfloat16 or wider, within the bound.
A program may use at most 64 MiB of HBM per device.

v0:
```python
import math
import jax
import jax.numpy as jnp
from jax import lax
from jax.sharding import PartitionSpec as P

plan_len = 1000


def noise_levels(timesteps):
    steps = jnp.arange(plan_len, dtype=jnp.float32)
    rooted = math.sqrt(0.00085) + (math.sqrt(0.012) - math.sqrt(0.00085)) * steps / (plan_len - 1)
    terms = jnp.log1p(-rooted * rooted)
    reached = jnp.arange(plan_len, dtype=jnp.int32) <= timesteps[..., None]
    picked = jnp.exp(jnp.sum(jnp.where(reached, terms, jnp.zeros_like(terms)), axis=-1))
    return (jnp.sqrt(picked), jnp.sqrt(1.0 - picked))


def gelu_parts(gate):
    cumul = 0.5 * (1.0 + jax.scipy.special.erf(gate / math.sqrt(2.0)))
    density = jnp.exp(-0.5 * gate * gate) / math.sqrt(2.0 * math.pi)
    return (gate * cumul, cumul + gate * density)


def contract_back(delta, weight):
    return lax.dot_general(
        delta, weight, (((1,), (1,)), ((), ())), preferred_element_type=jnp.float32
    )


def block_forward(residual_stream, weights, scale_gain, shift_bias):
    weight_in, weight_ffin, weight_ffout, weight_out = weights
    hidden = weight_ffout.shape[0]
    residual_reduced = residual_stream.astype(jnp.bfloat16)
    inner = jnp.dot(residual_reduced, weight_in, preferred_element_type=jnp.float32)
    centred_input = inner - jnp.mean(inner, axis=-1, keepdims=True)
    inverse_deviation = lax.rsqrt(
        jnp.mean(centred_input * centred_input, axis=-1, keepdims=True) + 1e-05
    )
    standardized_input = centred_input * inverse_deviation
    normalized_input = (standardized_input * scale_gain + shift_bias).astype(jnp.bfloat16)
    projected = jnp.dot(normalized_input, weight_ffin, preferred_element_type=jnp.float32)
    value_output = projected[:, :hidden]
    gate = projected[:, hidden:]
    gelu_result, gelu_derivative = gelu_parts(gate)
    mixed_hidden = (value_output * gelu_result).astype(jnp.bfloat16)
    inner_two = inner + jnp.dot(mixed_hidden, weight_ffout, preferred_element_type=jnp.float32)
    inner_reduced = inner_two.astype(jnp.bfloat16)
    residual_stream = residual_stream + jnp.dot(
        inner_reduced, weight_out, preferred_element_type=jnp.float32
    )
    return (
        residual_stream,
        (
            residual_reduced,
            standardized_input,
            inverse_deviation,
            normalized_input,
            value_output,
            gelu_result,
            gelu_derivative,
            mixed_hidden,
            inner_reduced,
        ),
    )


def block_backward(dstream, saved_activations, weights, scale_gain):
    weight_in, weight_ffin, weight_ffout, weight_out = weights
    (
        residual_reduced,
        standardized_input,
        inverse_deviation,
        normalized_input,
        value_output,
        gelu_result,
        gelu_derivative,
        mixed_hidden,
        inner_reduced,
    ) = saved_activations
    dout_low = dstream.astype(jnp.bfloat16)
    second_inner_gradient = contract_back(dout_low, weight_out)
    dtwo_low = second_inner_gradient.astype(jnp.bfloat16)
    dmixed = contract_back(dtwo_low, weight_ffout)
    dproj_low = jnp.concatenate(
        [dmixed * gelu_result, dmixed * value_output * gelu_derivative], axis=-1
    ).astype(jnp.bfloat16)
    dnormed = contract_back(dproj_low, weight_ffin)
    scaled_hidden = dnormed * scale_gain
    inner_gradient = second_inner_gradient + inverse_deviation * (
        scaled_hidden
        - jnp.mean(scaled_hidden, axis=-1, keepdims=True)
        - standardized_input * jnp.mean(scaled_hidden * standardized_input, axis=-1, keepdims=True)
    )
    dinner_low = inner_gradient.astype(jnp.bfloat16)
    dstream = dstream + contract_back(dinner_low, weight_in)
    records = [
        (residual_reduced, dinner_low),
        (normalized_input, dproj_low),
        (mixed_hidden, dtwo_low),
        (inner_reduced, dout_low),
    ]
    return (dstream, records)


def project_layer(inputs, deltas, sketch_in, sketch_out, samples):
    left = jnp.dot(inputs, sketch_in, preferred_element_type=jnp.float32)
    right = jnp.dot(deltas, sketch_out, preferred_element_type=jnp.float32)
    left = left.reshape(samples, -1, left.shape[-1])
    right = right.reshape(samples, -1, right.shape[-1])
    outer = jnp.einsum("srk,srj->skj", left, right, precision=lax.Precision.HIGHEST)
    return outer.reshape(samples, -1)


def sketches_of(block, sketch_cin, sketch_fin, sketch_cout, sketch_fout):
    return [
        (sketch_cin[block, 0], sketch_cout[block, 0]),
        (sketch_cin[block, 1], sketch_fout[block]),
        (sketch_fin[block], sketch_cout[block, 1]),
        (sketch_cin[block, 2], sketch_cout[block, 2]),
    ]


def on_device(
    clean_feats,
    noise_draw,
    timesteps,
    weight_in,
    weight_ffin,
    weight_ffout,
    weight_out,
    norm_gain,
    norm_bias,
    sketch_cin,
    sketch_fin,
    sketch_cout,
    sketch_fout,
    precond,
    store_grads,
    store_scale,
):
    samples = clean_feats.shape[0]
    positions = clean_feats.shape[2] * lax.axis_size("corpus")
    loss_scale = 1.0 / math.sqrt(clean_feats.shape[1] * positions)
    blocks = weight_in.shape[0]
    signal, spread = noise_levels(timesteps)
    noise_rows = noise_draw.astype(jnp.float32)
    residual_stream = (
        signal[:, :, None, None] * clean_feats.astype(jnp.float32)
        + spread[:, :, None, None] * noise_rows
    )
    residual_stream = residual_stream.reshape(-1, residual_stream.shape[-1])
    noise_rows = noise_rows.reshape(-1, noise_rows.shape[-1])
    gathered = (
        lax.all_gather(weight_in, "corpus", axis=2, tiled=True),
        lax.all_gather(weight_ffin, "corpus", axis=2, tiled=True),
        lax.all_gather(weight_ffout, "corpus", axis=2, tiled=True),
        lax.all_gather(weight_out, "corpus", axis=2, tiled=True),
    )

    def fetch_forward(block):
        return tuple((member[block] for member in gathered))

    def fetch_backward(block):
        return tuple((member[block] for member in gathered))

    saved_all = []
    for block in range(blocks):
        residual_stream, saved_activations = block_forward(
            residual_stream, fetch_forward(block), norm_gain[block], norm_bias[block]
        )
        saved_all.append(saved_activations)
    dstream = (residual_stream - noise_rows) * loss_scale
    layers = [None] * (4 * blocks)
    for block in reversed(range(blocks)):
        dstream, records = block_backward(
            dstream, saved_all[block], fetch_backward(block), norm_gain[block]
        )
        pairs = sketches_of(block, sketch_cin, sketch_fin, sketch_cout, sketch_fout)
        for index in range(4):
            layers[4 * block + index] = project_layer(
                records[index][0], records[index][1], pairs[index][0], pairs[index][1], samples
            )
    partial_grads = jnp.stack(layers, axis=1)
    totals = lax.psum(partial_grads, "corpus")
    routed = lax.all_to_all(totals, "query", split_axis=1, concat_axis=0, tiled=True)
    owned = jnp.einsum("qlk,lkj->qlj", routed, precond, precision=lax.Precision.HIGHEST).astype(
        jnp.bfloat16
    )
    preconditioned = lax.all_gather(owned, "query", axis=1, tiled=True)
    flat = preconditioned.reshape(preconditioned.shape[0], -1)
    raw = lax.dot_general(
        flat, store_grads, (((1,), (1,)), ((), ())), preferred_element_type=jnp.float32
    )
    return raw * store_scale[None, :]


def solution(mesh):
    placed = (
        P("query", None, "corpus", None),
        P("query", None, "corpus", None),
        P("query", None),
        P(None, None, "corpus"),
        P(None, None, "corpus"),
        P(None, None, "corpus"),
        P(None, None, "corpus"),
        P(),
        P(),
        P(),
        P(),
        P(),
        P(),
        P("query", None, None),
        P(("query", "corpus"), None),
        P(("query", "corpus")),
    )
    return jax.shard_map(
        on_device,
        mesh=mesh,
        in_specs=placed,
        out_specs=P(None, ("query", "corpus")),
        check_vma=False,
    )
```

profile of v0, /device:TPU:0, one launch (start us, length us, event | category | flops | bytes accessed | tf_op | source)
XLA Modules:
  0.0 167.8 jit_solution(465755251760985908)
XLA Ops:
  6.5 0.7 all-gather.5.cloned.1.call-update
  7.3 0.7 all-gather.3.cloned.1.call-update
  8.0 25.0 %all_gather.15 = bf16[2,320,320]{1,0,2:T(2,128)(2,1)S(1)} all-gather(bf16[2,320,20]{1,0,2:T(2,128)(2,1)} %param.19), channel_id=1, replica_groups=mesh['query'=2,'corpus'=16] {'corpus'}, dimensions={2}, use_global_device_ids=true | all-gather | bytes 435200 | tf_op jit(solution)/shard_map/all_gather | solution.py:155
  33.0 0.7 fusion.105
  33.7 0.9 copy.52
  34.6 19.7 %all_gather.18 = bf16[2,320,320]{1,0,2:T(2,128)(2,1)S(1)} all-gather(bf16[2,320,20]{1,0,2:T(2,128)(2,1)S(1)} %copy-done.12), channel_id=1, replica_groups=mesh['query'=2,'corpus'=16] {'corpus'}, dimensions={2}, use_global_device_ids=true | all-gather | bytes 435200 | tf_op jit(solution)/shard_map/all_gather | solution.py:158
  54.3 0.7 fusion.104
  55.0 0.9 copy.54
  55.9 0.9 copy.55
  56.8 0.9 copy.57
  57.7 0.6 slice_reduce_fusion
  58.3 0.2 fusion.93
  58.6 0.7 fusion.102
  59.3 0.3 fusion.106
  59.6 0.2 multiply_reduce_fusion.3
  59.8 0.8 fusion.79
  60.7 0.6 copy-done.4
  61.3 0.8 fusion.76
  62.2 5.7 %fusion.103 = (bf16[1,1280,320]{1,0,2:T(2,128)(2,1)}, bf16[1,1280,320]{1,0,2:T(2,128)(2,1)S(1)}) fusion(bf16[2,1280,320]{1,0,2:T(2,128)(2,1)} %all-gather.5.cloned.1.call-done), kind=kLoop, calls=%fused_computation.161 | loop fusion | bytes 3276800 | tf_op jit(solution)/shard_map/slice | solution.py:162
  67.9 36.5 %all-gather.3.cloned.1.call-done = bf16[2,320,2560]{1,2,0:T(8,128)(2,1)} async-done(((bf16[2,320,160]{1,2,0:T(8,128)(2,1)}), bf16[2,320,2560]{1,2,0:T(8,128)(2,1)}) %all-gather.3.cloned.1.call-update) | async-done | bytes 3276816 | tf_op jit(solution)/shard_map/all_gather | solution.py:156
  104.3 2.5 %fusion.1 = f32[64,2560]{1,0:T(8,128)S(1)} fusion(bf16[64,320]{1,0:T(8,128)(2,1)} %copy-done.4, bf16[2,320,2560]{1,2,0:T(8,128)(2,1)} %all-gather.3.cloned.1.call-done), kind=kOutput, calls=%fused_computation.3 | convolution fusion | flops 104857600 | bytes 2670592 | tf_op jit(solution)/shard_map/dot_general | solution.py:42
  106.9 0.4 fusion.8
  107.3 0.1 fusion.73
  107.4 0.2 convolution_add_fusion.4
  107.6 0.3 fusion.107
  107.9 0.2 multiply_reduce_fusion.2
  108.2 0.7 fusion.3
  109.0 0.3 copy-done.2
  109.3 0.4 fusion.9
  109.7 0.2 fusion.7
  109.9 0.2 fusion.26
  110.1 0.3 multiply_convert_fusion.1
  110.4 0.5 fusion.101
  111.0 0.1 add_convert_fusion.1
  111.1 0.2 fusion.10
  111.3 0.2 fusion.32
  111.5 0.3 multiply_convert_fusion
  111.8 0.1 fusion.50
  112.0 0.1 fusion.71
  112.1 0.1 fusion.59
  112.2 0.1 fusion.68
  112.4 0.1 fusion.66
  112.5 0.1 fusion.46
  112.6 0.2 fusion.44
  112.8 0.2 fusion.53
  113.0 0.1 fusion.63
  113.1 0.1 fusion.56
  113.3 0.2 fusion.38
  113.5 0.2 fusion.37
  113.7 0.5 fusion.100
  114.3 0.2 fusion.43
  114.5 0.1 fusion.108
  114.7 0.1 fusion.109
  114.9 0.1 fusion.110
  115.2 0.1 fusion.111
  115.4 0.1 fusion.112
  115.6 0.1 fusion.113
  115.8 0.1 fusion.114
  116.0 0.1 fusion.115
  116.3 32.2 %psum.7 = f32[1,8,256]{2,0,1:T(1,128)S(1)} all-reduce(f32[1,8,256]{2,0,1:T(1,128)S(1)} %constant_dynamic-update-slice_fusion), channel_id=1, replica_groups=mesh['query'=2,'corpus'=16] {'corpus'}, use_global_device_ids=true, to_apply=%region_9.10 | all-reduce | flops 2048 | bytes 16384 | tf_op jit(solution)/shard_map/psum | solution.py:185
  148.6 6.3 %all_to_all.12 = f32[1,8,256]{2,0,1:T(1,128)S(1)} all-to-all(f32[1,8,256]{2,0,1:T(1,128)S(1)} %psum.7), channel_id=1, replica_groups=mesh['query'=2,'corpus'=16] {'query'}, dimensions={1} | all-to-all | bytes 16384 | tf_op jit(solution)/shard_map/all_to_all | solution.py:186
  155.0 0.6 fusion.11
  155.6 4.3 %all_gather.19 = bf16[2,8,256]{2,0,1:T(2,128)(2,1)S(1)} all-gather(bf16[2,4,256]{2,0,1:T(2,128)(2,1)S(1)} %fusion.11), channel_id=1, replica_groups=mesh['query'=2,'corpus'=16] {'query'}, dimensions={1}, use_global_device_ids=true | all-gather | bytes 12288 | tf_op jit(solution)/shard_map/all_gather | solution.py:190
  160.0 1.0 convolution_multiply_fusion
  (79 shorter events, 1.4 us)
Async XLA Ops:
  6.5 148.5 %copy-start = (f32[4,256,256]{2,1,0:T(8,128)S(1)}, f32[4,256,256]{2,1,0:T(8,128)}, u32[]{:S(2)}) copy-start(f32[4,256,256]{2,1,0:T(8,128)} %param.29) | copy-start | bytes 3145732
  6.5 28.1 %copy-start.12 = (bf16[2,320,20]{1,0,2:T(2,128)(2,1)S(1)}, bf16[2,320,20]{1,0,2:T(2,128)(2,1)}, u32[]{:S(2)}) copy-start(bf16[2,320,20]{1,0,2:T(2,128)(2,1)} %param.22) | copy-start | bytes 76804
  6.5 55.6 %all-gather.5.cloned.1.call-start = ((), (), s32[]{:S(2)}) async-start(), calls=%async_computation.2 | async-start | bytes 1740800 | tf_op jit(solution)/shard_map/all_gather | solution.py:157
  7.3 97.1 %all-gather.3.cloned.1.call-start = ((), (), s32[]{:S(2)}) async-start(), calls=%async_computation.1 | async-start | bytes 4177920 | tf_op jit(solution)/shard_map/all_gather | solution.py:156
  54.3 3.4 %copy-start.16 = (f32[2,320]{1,0:T(2,128)S(1)}, f32[2,320]{1,0:T(2,128)}, u32[]{:S(2)}) copy-start(f32[2,320]{1,0:T(2,128)} %param.24) | copy-start | bytes 7684
  54.3 4.0 %copy-start.17 = (f32[2,320]{1,0:T(2,128)S(1)}, f32[2,320]{1,0:T(2,128)}, u32[]{:S(2)}) copy-start(f32[2,320]{1,0:T(2,128)} %param.23) | copy-start | bytes 7684
  54.3 4.0 %copy-start.21 = (s32[1,2]{1,0:T(1,128)S(1)}, s32[1,2]{1,0:T(1,128)}, u32[]{:S(2)}) copy-start(s32[1,2]{1,0:T(1,128)} %param.18) | copy-start | bytes 28
  54.3 4.3 %copy-start.6 = (bf16[1,2,32,320]{3,2,1,0:T(8,128)(2,1)S(1)}, bf16[1,2,32,320]{3,2,1,0:T(8,128)(2,1)}, u32[]{:S(2)}) copy-start(bf16[1,2,32,320]{3,2,1,0:T(8,128)(2,1)} %param.17) | copy-start | bytes 122884
  54.3 4.3 %copy-start.11 = (bf16[1,2,32,320]{3,2,1,0:T(8,128)(2,1)S(1)}, bf16[1,2,32,320]{3,2,1,0:T(8,128)(2,1)}, u32[]{:S(2)}) copy-start(bf16[1,2,32,320]{3,2,1,0:T(8,128)(2,1)} %param.16) | copy-start | bytes 122884
  59.6 8.3 %copy-start.14 = (f32[64]{0:T(128)}, f32[64]{0:T(128)S(1)}, u32[]{:S(2)}) copy-start(f32[64]{0:T(128)S(1)} %broadcast_multiply_fusion.5) | copy-start | bytes 772
  59.8 2.4 %copy-start.18 = (f32[64]{0:T(128)}, f32[64]{0:T(128)S(1)}, u32[]{:S(2)}) copy-start(f32[64]{0:T(128)S(1)} %add_rsqrt_fusion.1) | copy-start | bytes 772
  60.7 0.6 copy-start.4
  104.3 2.9 %copy-start.10 = (bf16[2,3,320,16]{2,3,1,0:T(8,128)(2,1)S(1)}, bf16[2,3,320,16]{2,3,1,0:T(8,128)(2,1)}, u32[]{:S(2)}) copy-start(bf16[2,3,320,16]{2,3,1,0:T(8,128)(2,1)} %param.25) | copy-start | bytes 184324
  104.3 3.1 %copy-start.5 = (f32[1,2,32,320]{3,2,1,0:T(8,128)S(1)}, f32[1,2,32,320]{3,2,1,0:T(8,128)}, u32[]{:S(2)}) copy-start(f32[1,2,32,320]{3,2,1,0:T(8,128)} %get-tuple-element.14) | copy-start | bytes 245764
  104.3 3.9 %copy-start.1 = (bf16[2,320,2560]{1,2,0:T(8,128)(2,1)S(1)}, bf16[2,320,2560]{1,2,0:T(8,128)(2,1)}, u32[]{:S(2)}) copy-start(bf16[2,320,2560]{1,2,0:T(8,128)(2,1)} %all-gather.3.cloned.1.call-done) | copy-start | bytes 9830404
  106.8 1.3 copy-start.13
  107.9 1.4 copy-start.2
  108.2 1.5 copy-start.7
  110.9 0.9 copy-start.9
  110.9 1.6 copy-start.8
  111.3 2.0 %copy-start.22 = (bf16[2,2560,16]{1,2,0:T(8,128)(2,1)S(1)}, bf16[2,2560,16]{1,2,0:T(8,128)(2,1)}, u32[]{:S(2)}) copy-start(bf16[2,2560,16]{1,2,0:T(8,128)(2,1)} %param.28) | copy-start | bytes 491524
  111.5 2.2 %copy-start.15 = (f32[64]{0:T(128)S(1)}, f32[64]{0:T(128)}, u32[]{:S(2)}) copy-start(f32[64]{0:T(128)} %copy-done.14) | copy-start | bytes 772
  111.5 2.2 %copy-start.19 = (f32[64]{0:T(128)S(1)}, f32[64]{0:T(128)}, u32[]{:S(2)}) copy-start(f32[64]{0:T(128)} %copy-done.18) | copy-start | bytes 772
  113.7 46.3 %copy-start.3 = (bf16[256,2048]{1,0:T(8,128)(2,1)S(1)}, bf16[256,2048]{1,0:T(8,128)(2,1)}, u32[]{:S(2)}) copy-start(bf16[256,2048]{1,0:T(8,128)(2,1)} %param.30) | copy-start | bytes 3145732
  113.7 46.3 %copy-start.20 = (f32[256]{0:T(256)S(1)}, f32[256]{0:T(256)}, u32[]{:S(2)}) copy-start(f32[256]{0:T(256)} %param.31) | copy-start | bytes 3076
Sparse Core Ops, SparseCore 0:
  9.5 43.8 all-gather.4
  55.7 48.5 all-gather.2
where the time goes:
time: 168 us
  blocking collectives  87.6 us (52%)
  waiting for transfers between devices  37.9 us (23%)
  between operations  13.9 us (8%)
  matrix products  13.5 us (8%)
  local copies, waits for them, and re-layouts  13 us (8%)
  other arithmetic  1.84 us (1%)
    all_gather x1, waiting for transfers between devices, on_device(): lax.all_gather(weight_ffin, 'corpus', axis=2, tiled=True)  36.5 us
    psum x1, blocking collectives, on_device(): totals = lax.psum(partial_grads, 'corpus')  32.2 us
    all_gather x1, blocking collectives, on_device(): lax.all_gather(weight_in, 'corpus', axis=2, tiled=True)  25 us
    all_gather x1, blocking collectives, on_device(): lax.all_gather(weight_out, 'corpus', axis=2, tiled=True)  19.7 us
    slice x3, local copies, waits for them, and re-layouts, fetch_forward(): return tuple((member[block] for member in gathered))  7.04 us
    all_to_all x1, blocking collectives, on_device(): lax.all_to_all(totals, 'query', split_axis=1, concat_axis=0, tiled=True)  6.35 us
    unnamed x57, local copies, waits for them, and re-layouts  4.61 us
    all_gather x1, blocking collectives, on_device(): preconditioned = lax.all_gather(owned, 'query', axis=1, tiled=True)  4.33 us
  transfers between devices with their start and end apart: 2, of which 1 were waited for; matrix products, arithmetic and copies ran while one was open for 9% of the time, Pallas kernels for 0%

commit v1 on v0

--- a/solution.py
+++ b/solution.py
@@ -3,8 +3,31 @@
 import jax.numpy as jnp
 from jax import lax
 from jax.sharding import PartitionSpec as P
+from jax.lax import axis_index, axis_size, ppermute
 
 plan_len = 1000
+
+
+def point_series(mesh_dim, shard_in):
+    res = axis_size(mesh_dim)
+    base_arr, before, w1 = (res, axis_index(mesh_dim), shard_in.shape[2])
+    runs = tuple(((at, (at + 1) % base_arr) for at in range(base_arr)))
+    column = tuple(((at, (at - 1) % base_arr) for at in range(base_arr)))
+    f_now = jnp.zeros((*shard_in.shape[:2], base_arr * w1, *shard_in.shape[3:]), shard_in.dtype)
+    f_now = lax.dynamic_update_slice_in_dim(f_now, shard_in, before * w1, axis=2)
+    carry_out = n_now = shard_in
+    found_now = base_arr // 2
+    for p in [*range(1, found_now + 1)]:
+        carry_out = ppermute(carry_out, mesh_dim, runs)
+        f_now = lax.dynamic_update_slice_in_dim(
+            f_now, carry_out, (before - p) % base_arr * w1, axis=2
+        )
+        if p < base_arr - found_now:
+            n_now = ppermute(n_now, mesh_dim, column)
+            f_now = lax.dynamic_update_slice_in_dim(
+                f_now, n_now, (before + p) % base_arr * w1, axis=2
+            )
+    return f_now
 
 
 def noise_levels(timesteps):
@@ -153,7 +176,7 @@
     noise_rows = noise_rows.reshape(-1, noise_rows.shape[-1])
     gathered = (
         lax.all_gather(weight_in, "corpus", axis=2, tiled=True),
-        lax.all_gather(weight_ffin, "corpus", axis=2, tiled=True),
+        point_series("corpus", weight_ffin),
         lax.all_gather(weight_ffout, "corpus", axis=2, tiled=True),
         lax.all_gather(weight_out, "corpus", axis=2, tiled=True),
     )

time: 168 us -> 186 us (1.11)
  starting transfers between devices: 0.04 us -> 32.3 us
  waiting for transfers between devices: 37.9 us -> 29.9 us
  blocking collectives: 87.6 us -> 81 us
  matrix products: 13.5 us -> 10.3 us
  local copies, waits for them, and re-layouts: 13 us -> 15.3 us
    all_gather x1 -> x0, waiting for transfers between devices: 36.5 us -> none  [on_device(): lax.all_gather(weight_ffin, 'corpus', axis=2, tiled=True)]
    ppermute x0 -> x15, starting transfers between devices: none -> 32.2 us  [the longest x7 31.4 us: point_series(): n_now = ppermute(n_now, mesh_dim, column)]
    ppermute x0 -> x15, waiting for transfers between devices: none -> 29.8 us  [the longest x8 29.8 us: point_series(): carry_out = ppermute(carry_out, mesh_dim, runs)]
    all_gather x1, blocking collectives: 25 us -> 21.2 us  [on_device(): lax.all_gather(weight_in, 'corpus', axis=2, tiled=True)]
    dynamic_update_slice x0 -> x16, local copies, waits for them, and re-layouts: none -> 2.57 us  [the longest x7 1.26 us: point_series(): lax.dynamic_update_slice_in_dim(f_now, n_now, (before + p) % base_arr * w...]
    psum x1, blocking collectives: 32.2 us -> 30 us  [on_device(): totals = lax.psum(partial_grads, 'corpus')]
    unnamed x57 -> x39, local copies, waits for them, and re-layouts: 4.61 us -> 5.54 us
  transfers between devices with their start and end apart: 2 -> 16, of which waited for: 1 -> 7; matrix products, arithmetic and copies ran while one was open for 9% -> 6% of each run, Pallas kernels for 0% -> 0%
where the time goes in v1:
time: 186 us
  blocking collectives  81 us (44%)
  starting transfers between devices  32.3 us (17%)
  waiting for transfers between devices  29.9 us (16%)
  local copies, waits for them, and re-layouts  15.3 us (8%)
  between operations  14.3 us (8%)
  matrix products  10.3 us (6%)
  other arithmetic  2.66 us (1%)
    ppermute x7, starting transfers between devices, point_series(): n_now = ppermute(n_now, mesh_dim, column)  31.4 us
    psum x1, blocking collectives, on_device(): totals = lax.psum(partial_grads, 'corpus')  30 us
    ppermute x8, waiting for transfers between devices, point_series(): carry_out = ppermute(carry_out, mesh_dim, runs)  29.8 us
    all_gather x1, blocking collectives, on_device(): lax.all_gather(weight_in, 'corpus', axis=2, tiled=True)  21.2 us
    all_gather x1, blocking collectives, on_device(): lax.all_gather(weight_out, 'corpus', axis=2, tiled=True)  19.1 us
    all_to_all x1, blocking collectives, on_device(): lax.all_to_all(totals, 'query', split_axis=1, concat_axis=0, tiled=True)  6.36 us
    slice x3, local copies, waits for them, and re-layouts, fetch_forward(): return tuple((member[block] for member in gathered))  6.1 us
    unnamed x39, local copies, waits for them, and re-layouts  5.54 us
  transfers between devices with their start and end apart: 16, of which 7 were waited for; matrix products, arithmetic and copies ran while one was open for 6% of the time, Pallas kernels for 0%

profile of v1, /device:TPU:0, one launch (start us, length us, event | category | flops | bytes accessed | tf_op | source)
XLA Modules:
  0.0 185.8 jit_solution(10408542153390276865)
XLA Ops:
  6.6 0.5 collective-permute-start
  7.1 5.1 %collective-permute-start.1 = (bf16[2,320,160]{1,2,0:T(8,128)(2,1)}, bf16[2,320,160]{1,2,0:T(8,128)(2,1)}, u32[]{:S(2)}, u32[]{:S(2)}) collective-permute-start(bf16[2,320,160]{1,2,0:T(8,128)(2,1)} %param.20), channel_id=1, source_target_pairs={{0,15},{1,0},{2,1},{3,2},{4,3},{5,4},{6,5},{7,6},{8,7},{9,8},{10,9... | collective-permute-start | bytes 614408 | tf_op jit(solution)/shard_map/ppermute | solution.py:26
  12.5 0.8 fusion.93
  13.3 21.2 %all_gather.12 = bf16[2,320,320]{1,0,2:T(2,128)(2,1)S(1)} all-gather(bf16[2,320,20]{1,0,2:T(2,128)(2,1)} %param.19), channel_id=1, replica_groups=mesh['query'=2,'corpus'=16] {'corpus'}, dimensions={2}, use_global_device_ids=true | all-gather | bytes 435200 | tf_op jit(solution)/shard_map/all_gather | solution.py:178
  34.6 0.7 fusion.105
  35.2 0.9 copy.52
  36.1 0.9 fusion.102
  37.2 0.3 fusion.106
  37.5 0.2 multiply_reduce_fusion.3
  37.7 19.1 %all_gather.14 = bf16[2,320,320]{1,0,2:T(2,128)(2,1)S(1)} all-gather(bf16[2,320,20]{1,0,2:T(2,128)(2,1)S(1)} %copy-done.9), channel_id=1, replica_groups=mesh['query'=2,'corpus'=16] {'corpus'}, dimensions={2}, use_global_device_ids=true | all-gather | bytes 435200 | tf_op jit(solution)/shard_map/all_gather | solution.py:181
  56.8 0.7 fusion.104
  57.5 0.9 copy.54
  58.4 0.9 copy.55
  59.3 0.9 copy.57
  60.4 0.3 broadcast_in_dim.12
  60.9 0.4 collective-permute-start.2
  61.3 4.1 %collective-permute-start.3 = (bf16[2,320,160]{1,2,0:T(8,128)(2,1)}, bf16[2,320,160]{1,2,0:T(8,128)(2,1)S(1)}, u32[]{:S(2)}, u32[]{:S(2)}) collective-permute-start(bf16[2,320,160]{1,2,0:T(8,128)(2,1)} %collective-permute-done.1), channel_id=1, source_target_pairs={{0,15},{1,0},{2,1},{3,2},{4,3},{5,4},{6,5},{7,6},{8,7},{9,8},{10,9... | collective-permute-start | bytes 614408 | tf_op jit(solution)/shard_map/ppermute | solution.py:26
  65.4 1.0 constant_dynamic-update-slice_fusion.22
  66.4 1.0 constant_dynamic-update-slice_fusion.21
  67.4 2.2 %collective-permute-done.2 = bf16[2,320,160]{1,2,0:T(8,128)(2,1)S(1)} collective-permute-done((bf16[2,320,160]{1,2,0:T(8,128)(2,1)}, bf16[2,320,160]{1,2,0:T(8,128)(2,1)S(1)}, u32[]{:S(2)}, u32[]{:S(2)}) %collective-permute-start.2) | collective-permute-done | bytes 204832 | tf_op jit(solution)/shard_map/ppermute | solution.py:21
  69.6 4.4 %collective-permute-start.5 = (bf16[2,320,160]{1,2,0:T(8,128)(2,1)S(1)}, bf16[2,320,160]{1,2,0:T(8,128)(2,1)S(1)}, u32[]{:S(2)}, u32[]{:S(2)}) collective-permute-start(bf16[2,320,160]{1,2,0:T(8,128)(2,1)S(1)} %collective-permute-done.3), channel_id=1, source_target_pairs={{0,15},{1,0},{2,1},{3,2},{4,3},{5,4},{6,5},{7,6},{8,7},{9,8},{10,9... | collective-permute-start | bytes 614408 | tf_op jit(solution)/shard_map/ppermute | solution.py:26
  74.1 3.9 %collective-permute-done.4 = bf16[2,320,160]{1,2,0:T(8,128)(2,1)S(1)} collective-permute-done((bf16[2,320,160]{1,2,0:T(8,128)(2,1)S(1)}, bf16[2,320,160]{1,2,0:T(8,128)(2,1)S(1)}, u32[]{:S(2)}, u32[]{:S(2)}) %collective-permute-start.4) | collective-permute-done | bytes 204832 | tf_op jit(solution)/shard_map/ppermute | solution.py:21
  78.0 4.4 %collective-permute-start.7 = (bf16[2,320,160]{1,2,0:T(8,128)(2,1)S(1)}, bf16[2,320,160]{1,2,0:T(8,128)(2,1)S(1)}, u32[]{:S(2)}, u32[]{:S(2)}) collective-permute-start(bf16[2,320,160]{1,2,0:T(8,128)(2,1)S(1)} %collective-permute-done.5), channel_id=1, source_target_pairs={{0,15},{1,0},{2,1},{3,2},{4,3},{5,4},{6,5},{7,6},{8,7},{9,8},{10,9... | collective-permute-start | bytes 614408 | tf_op jit(solution)/shard_map/ppermute | solution.py:26
  82.6 3.9 %collective-permute-done.6 = bf16[2,320,160]{1,2,0:T(8,128)(2,1)S(1)} collective-permute-done((bf16[2,320,160]{1,2,0:T(8,128)(2,1)S(1)}, bf16[2,320,160]{1,2,0:T(8,128)(2,1)S(1)}, u32[]{:S(2)}, u32[]{:S(2)}) %collective-permute-start.6) | collective-permute-done | bytes 204832 | tf_op jit(solution)/shard_map/ppermute | solution.py:21
  86.4 4.4 %collective-permute-start.9 = (bf16[2,320,160]{1,2,0:T(8,128)(2,1)S(1)}, bf16[2,320,160]{1,2,0:T(8,128)(2,1)S(1)}, u32[]{:S(2)}, u32[]{:S(2)}) collective-permute-start(bf16[2,320,160]{1,2,0:T(8,128)(2,1)S(1)} %collective-permute-done.7), channel_id=1, source_target_pairs={{0,15},{1,0},{2,1},{3,2},{4,3},{5,4},{6,5},{7,6},{8,7},{9,8},{10,9... | collective-permute-start | bytes 614408 | tf_op jit(solution)/shard_map/ppermute | solution.py:26
  91.0 3.9 %collective-permute-done.8 = bf16[2,320,160]{1,2,0:T(8,128)(2,1)S(1)} collective-permute-done((bf16[2,320,160]{1,2,0:T(8,128)(2,1)S(1)}, bf16[2,320,160]{1,2,0:T(8,128)(2,1)S(1)}, u32[]{:S(2)}, u32[]{:S(2)}) %collective-permute-start.8) | collective-permute-done | bytes 204832 | tf_op jit(solution)/shard_map/ppermute | solution.py:21
  94.9 4.4 %collective-permute-start.11 = (bf16[2,320,160]{1,2,0:T(8,128)(2,1)S(1)}, bf16[2,320,160]{1,2,0:T(8,128)(2,1)S(1)}, u32[]{:S(2)}, u32[]{:S(2)}) collective-permute-start(bf16[2,320,160]{1,2,0:T(8,128)(2,1)S(1)} %collective-permute-done.9), channel_id=1, source_target_pairs={{0,15},{1,0},{2,1},{3,2},{4,3},{5,4},{6,5},{7,6},{8,7},{9,8},{10,9... | collective-permute-start | bytes 614408 | tf_op jit(solution)/shard_map/ppermute | solution.py:26
  99.4 3.9 %collective-permute-done.10 = bf16[2,320,160]{1,2,0:T(8,128)(2,1)S(1)} collective-permute-done((bf16[2,320,160]{1,2,0:T(8,128)(2,1)S(1)}, bf16[2,320,160]{1,2,0:T(8,128)(2,1)S(1)}, u32[]{:S(2)}, u32[]{:S(2)}) %collective-permute-start.10) | collective-permute-done | bytes 204832 | tf_op jit(solution)/shard_map/ppermute | solution.py:21
  103.3 4.4 %collective-permute-start.13 = (bf16[2,320,160]{1,2,0:T(8,128)(2,1)S(1)}, bf16[2,320,160]{1,2,0:T(8,128)(2,1)S(1)}, u32[]{:S(2)}, u32[]{:S(2)}) collective-permute-start(bf16[2,320,160]{1,2,0:T(8,128)(2,1)S(1)} %collective-permute-done.11), channel_id=1, source_target_pairs={{0,15},{1,0},{2,1},{3,2},{4,3},{5,4},{6,5},{7,6},{8,7},{9,8},{10,9... | collective-permute-start | bytes 614408 | tf_op jit(solution)/shard_map/ppermute | solution.py:26
  107.8 3.9 %collective-permute-done.12 = bf16[2,320,160]{1,2,0:T(8,128)(2,1)S(1)} collective-permute-done((bf16[2,320,160]{1,2,0:T(8,128)(2,1)S(1)}, bf16[2,320,160]{1,2,0:T(8,128)(2,1)S(1)}, u32[]{:S(2)}, u32[]{:S(2)}) %collective-permute-start.12) | collective-permute-done | bytes 204832 | tf_op jit(solution)/shard_map/ppermute | solution.py:21
  111.8 8.2 %collective-permute-done.14 = bf16[2,320,160]{1,2,0:T(8,128)(2,1)S(1)} collective-permute-done((bf16[2,320,160]{1,2,0:T(8,128)(2,1)S(1)}, bf16[2,320,160]{1,2,0:T(8,128)(2,1)S(1)}, u32[]{:S(2)}, u32[]{:S(2)}) %collective-permute-start.14) | collective-permute-done | bytes 204832 | tf_op jit(solution)/shard_map/ppermute | solution.py:21
  120.1 1.9 %copy-done.1 = bf16[2,320,2560]{1,2,0:T(8,128)(2,1)} copy-done((bf16[2,320,2560]{1,2,0:T(8,128)(2,1)}, bf16[2,320,2560]{1,2,0:T(8,128)(2,1)S(1)}, u32[]{:S(2)}) %copy-start.1) | copy-done | bytes 3276824
  122.0 0.7 fusion.1
  122.9 4.7 %fusion.103 = (bf16[1,1280,320]{1,0,2:T(2,128)(2,1)S(1)}, bf16[1,1280,320]{1,0,2:T(2,128)(2,1)S(1)}) fusion(bf16[2,1280,320]{1,0,2:T(2,128)(2,1)} %all-gather.2.cloned.1.call-done), kind=kLoop, calls=%fused_computation.177 | loop fusion | bytes 3276800 | tf_op jit(solution)/shard_map/slice | solution.py:185
  127.7 0.4 fusion.8
  128.2 0.2 convolution_add_fusion.4
  128.3 0.3 fusion.107
  128.6 0.2 multiply_reduce_fusion.2
  128.9 0.7 fusion.3
  129.8 0.4 fusion.9
  130.2 0.2 fusion.7
  130.3 0.2 fusion.26
  130.6 0.3 multiply_convert_fusion.1
  130.9 0.5 fusion.101
  131.5 0.2 fusion.10
  131.7 0.2 fusion.32
  131.9 0.3 multiply_convert_fusion
  132.5 0.1 fusion.59
  132.7 0.1 fusion.68
  132.8 0.1 fusion.66
  133.0 0.5 fusion.100
  133.5 0.2 fusion.37
  133.7 0.2 fusion.38
  133.9 0.1 fusion.44
  134.0 0.2 fusion.53
  134.2 0.1 fusion.63
  134.3 0.1 fusion.56
  134.5 0.2 fusion.43
  134.7 0.1 fusion.108
  136.6 30.0 %psum.7 = f32[1,8,256]{2,0,1:T(1,128)S(1)} all-reduce(f32[1,8,256]{2,0,1:T(1,128)S(1)} %constant_dynamic-update-slice_fusion), channel_id=1, replica_groups=mesh['query'=2,'corpus'=16] {'corpus'}, use_global_device_ids=true, to_apply=%region_9.10 | all-reduce | flops 2048 | bytes 16384 | tf_op jit(solution)/shard_map/psum | solution.py:208
  166.6 6.4 %all_to_all.12 = f32[1,8,256]{2,0,1:T(1,128)S(1)} all-to-all(f32[1,8,256]{2,0,1:T(1,128)S(1)} %psum.7), channel_id=1, replica_groups=mesh['query'=2,'corpus'=16] {'query'}, dimensions={1} | all-to-all | bytes 16384 | tf_op jit(solution)/shard_map/all_to_all | solution.py:209
  173.0 0.6 fusion.11
  173.6 4.3 %all_gather.15 = bf16[2,8,256]{2,0,1:T(2,128)(2,1)S(1)} all-gather(bf16[2,4,256]{2,0,1:T(2,128)(2,1)S(1)} %fusion.11), channel_id=1, replica_groups=mesh['query'=2,'corpus'=16] {'query'}, dimensions={1}, use_global_device_ids=true | all-gather | bytes 12288 | tf_op jit(solution)/shard_map/all_gather | solution.py:213
  178.0 1.0 convolution_multiply_fusion
  (105 shorter events, 3.8 us)
Async XLA Ops:
  6.5 166.5 %copy-start = (f32[4,256,256]{2,1,0:T(8,128)S(1)}, f32[4,256,256]{2,1,0:T(8,128)}, u32[]{:S(2)}) copy-start(f32[4,256,256]{2,1,0:T(8,128)} %param.29) | copy-start | bytes 3145732
  6.5 30.5 %copy-start.8 = (bf16[2,3,320,16]{2,3,1,0:T(8,128)(2,1)S(1)}, bf16[2,3,320,16]{2,3,1,0:T(8,128)(2,1)}, u32[]{:S(2)}) copy-start(bf16[2,3,320,16]{2,3,1,0:T(8,128)(2,1)} %param.25) | copy-start | bytes 184324
  6.5 30.9 %copy-start.10 = (f32[2,320]{1,0:T(2,128)S(1)}, f32[2,320]{1,0:T(2,128)}, u32[]{:S(2)}) copy-start(f32[2,320]{1,0:T(2,128)} %param.24) | copy-start | bytes 7684
  6.5 31.0 %copy-start.11 = (f32[2,320]{1,0:T(2,128)S(1)}, f32[2,320]{1,0:T(2,128)}, u32[]{:S(2)}) copy-start(f32[2,320]{1,0:T(2,128)} %param.23) | copy-start | bytes 7684
  6.5 31.2 %copy-start.9 = (bf16[2,320,20]{1,0,2:T(2,128)(2,1)S(1)}, bf16[2,320,20]{1,0,2:T(2,128)(2,1)}, u32[]{:S(2)}) copy-start(bf16[2,320,20]{1,0,2:T(2,128)(2,1)} %param.22) | copy-start | bytes 76804
  6.5 116.4 %all-gather.2.cloned.1.call-start = ((), (), s32[]{:S(2)}) async-start(), calls=%async_computation.1 | async-start | bytes 1740800 | tf_op jit(solution)/shard_map/all_gather | solution.py:180
  6.6 54.3 %collective-permute-start = (bf16[2,320,160]{1,2,0:T(8,128)(2,1)}, bf16[2,320,160]{1,2,0:T(8,128)(2,1)}, u32[]{:S(2)}, u32[]{:S(2)}) collective-permute-start(bf16[2,320,160]{1,2,0:T(8,128)(2,1)} %param.20), channel_id=1, source_target_pairs={{0,1},{1,2},{2,3},{3,4},{4,5},{5,6},{6,7},{7,8},{8,9},{9,10},{10,1... | collective-permute-start | bytes 614408 | tf_op jit(solution)/shard_map/ppermute | solution.py:21
  7.1 54.2 %collective-permute-start.1 = (bf16[2,320,160]{1,2,0:T(8,128)(2,1)}, bf16[2,320,160]{1,2,0:T(8,128)(2,1)}, u32[]{:S(2)}, u32[]{:S(2)}) collective-permute-start(bf16[2,320,160]{1,2,0:T(8,128)(2,1)} %param.20), channel_id=1, source_target_pairs={{0,15},{1,0},{2,1},{3,2},{4,3},{5,4},{6,5},{7,6},{8,7},{9,8},{10,9... | collective-permute-start | bytes 614408 | tf_op jit(solution)/shard_map/ppermute | solution.py:26
  56.8 3.9 %copy-start.4 = (bf16[2,320,160]{1,2,0:T(8,128)(2,1)S(1)}, bf16[2,320,160]{1,2,0:T(8,128)(2,1)}, u32[]{:S(2)}) copy-start(bf16[2,320,160]{1,2,0:T(8,128)(2,1)} %param.20) | copy-start | bytes 614404
  60.9 8.7 %collective-permute-start.2 = (bf16[2,320,160]{1,2,0:T(8,128)(2,1)}, bf16[2,320,160]{1,2,0:T(8,128)(2,1)S(1)}, u32[]{:S(2)}, u32[]{:S(2)}) collective-permute-start(bf16[2,320,160]{1,2,0:T(8,128)(2,1)} %collective-permute-done), channel_id=1, source_target_pairs={{0,1},{1,2},{2,3},{3,4},{4,5},{5,6},{6,7},{7,8},{8,9},{9,10},{10,1... | collective-permute-start | bytes 614408 | tf_op jit(solution)/shard_map/ppermute | solution.py:21
  61.3 8.3 %collective-permute-start.3 = (bf16[2,320,160]{1,2,0:T(8,128)(2,1)}, bf16[2,320,160]{1,2,0:T(8,128)(2,1)S(1)}, u32[]{:S(2)}, u32[]{:S(2)}) collective-permute-start(bf16[2,320,160]{1,2,0:T(8,128)(2,1)} %collective-permute-done.1), channel_id=1, source_target_pairs={{0,15},{1,0},{2,1},{3,2},{4,3},{5,4},{6,5},{7,6},{8,7},{9,8},{10,9... | collective-permute-start | bytes 614408 | tf_op jit(solution)/shard_map/ppermute | solution.py:26
  69.6 8.4 %collective-permute-start.4 = (bf16[2,320,160]{1,2,0:T(8,128)(2,1)S(1)}, bf16[2,320,160]{1,2,0:T(8,128)(2,1)S(1)}, u32[]{:S(2)}, u32[]{:S(2)}) collective-permute-start(bf16[2,320,160]{1,2,0:T(8,128)(2,1)S(1)} %collective-permute-done.2), channel_id=1, source_target_pairs={{0,1},{1,2},{2,3},{3,4},{4,5},{5,6},{6,7},{7,8},{8,9},{9,10},{10,1... | collective-permute-start | bytes 614408 | tf_op jit(solution)/shard_map/ppermute | solution.py:21
  69.6 8.4 %collective-permute-start.5 = (bf16[2,320,160]{1,2,0:T(8,128)(2,1)S(1)}, bf16[2,320,160]{1,2,0:T(8,128)(2,1)S(1)}, u32[]{:S(2)}, u32[]{:S(2)}) collective-permute-start(bf16[2,320,160]{1,2,0:T(8,128)(2,1)S(1)} %collective-permute-done.3), channel_id=1, source_target_pairs={{0,15},{1,0},{2,1},{3,2},{4,3},{5,4},{6,5},{7,6},{8,7},{9,8},{10,9... | collective-permute-start | bytes 614408 | tf_op jit(solution)/shard_map/ppermute | solution.py:26
  78.0 8.4 %collective-permute-start.6 = (bf16[2,320,160]{1,2,0:T(8,128)(2,1)S(1)}, bf16[2,320,160]{1,2,0:T(8,128)(2,1)S(1)}, u32[]{:S(2)}, u32[]{:S(2)}) collective-permute-start(bf16[2,320,160]{1,2,0:T(8,128)(2,1)S(1)} %collective-permute-done.4), channel_id=1, source_target_pairs={{0,1},{1,2},{2,3},{3,4},{4,5},{5,6},{6,7},{7,8},{8,9},{9,10},{10,1... | collective-permute-start | bytes 614408 | tf_op jit(solution)/shard_map/ppermute | solution.py:21
  78.0 8.4 %collective-permute-start.7 = (bf16[2,320,160]{1,2,0:T(8,128)(2,1)S(1)}, bf16[2,320,160]{1,2,0:T(8,128)(2,1)S(1)}, u32[]{:S(2)}, u32[]{:S(2)}) collective-permute-start(bf16[2,320,160]{1,2,0:T(8,128)(2,1)S(1)} %collective-permute-done.5), channel_id=1, source_target_pairs={{0,15},{1,0},{2,1},{3,2},{4,3},{5,4},{6,5},{7,6},{8,7},{9,8},{10,9... | collective-permute-start | bytes 614408 | tf_op jit(solution)/shard_map/ppermute | solution.py:26
  82.6 40.2 %copy-start.6 = (bf16[2,1280,16]{1,2,0:T(8,128)(2,1)S(1)}, bf16[2,1280,16]{1,2,0:T(8,128)(2,1)}, u32[]{:S(2)}) copy-start(bf16[2,1280,16]{1,2,0:T(8,128)(2,1)} %param.26) | copy-start | bytes 245764
  86.4 8.4 %collective-permute-start.8 = (bf16[2,320,160]{1,2,0:T(8,128)(2,1)S(1)}, bf16[2,320,160]{1,2,0:T(8,128)(2,1)S(1)}, u32[]{:S(2)}, u32[]{:S(2)}) collective-permute-start(bf16[2,320,160]{1,2,0:T(8,128)(2,1)S(1)} %collective-permute-done.6), channel_id=1, source_target_pairs={{0,1},{1,2},{2,3},{3,4},{4,5},{5,6},{6,7},{7,8},{8,9},{9,10},{10,1... | collective-permute-start | bytes 614408 | tf_op jit(solution)/shard_map/ppermute | solution.py:21
  86.4 8.4 %collective-permute-start.9 = (bf16[2,320,160]{1,2,0:T(8,128)(2,1)S(1)}, bf16[2,320,160]{1,2,0:T(8,128)(2,1)S(1)}, u32[]{:S(2)}, u32[]{:S(2)}) collective-permute-start(bf16[2,320,160]{1,2,0:T(8,128)(2,1)S(1)} %collective-permute-done.7), channel_id=1, source_target_pairs={{0,15},{1,0},{2,1},{3,2},{4,3},{5,4},{6,5},{7,6},{8,7},{9,8},{10,9... | collective-permute-start | bytes 614408 | tf_op jit(solution)/shard_map/ppermute | solution.py:26
  94.9 8.4 %collective-permute-start.10 = (bf16[2,320,160]{1,2,0:T(8,128)(2,1)S(1)}, bf16[2,320,160]{1,2,0:T(8,128)(2,1)S(1)}, u32[]{:S(2)}, u32[]{:S(2)}) collective-permute-start(bf16[2,320,160]{1,2,0:T(8,128)(2,1)S(1)} %collective-permute-done.8), channel_id=1, source_target_pairs={{0,1},{1,2},{2,3},{3,4},{4,5},{5,6},{6,7},{7,8},{8,9},{9,10},{10,1... | collective-permute-start | bytes 614408 | tf_op jit(solution)/shard_map/ppermute | solution.py:21
  94.9 8.4 %collective-permute-start.11 = (bf16[2,320,160]{1,2,0:T(8,128)(2,1)S(1)}, bf16[2,320,160]{1,2,0:T(8,128)(2,1)S(1)}, u32[]{:S(2)}, u32[]{:S(2)}) collective-permute-start(bf16[2,320,160]{1,2,0:T(8,128)(2,1)S(1)} %collective-permute-done.9), channel_id=1, source_target_pairs={{0,15},{1,0},{2,1},{3,2},{4,3},{5,4},{6,5},{7,6},{8,7},{9,8},{10,9... | collective-permute-start | bytes 614408 | tf_op jit(solution)/shard_map/ppermute | solution.py:26
  103.3 8.4 %collective-permute-start.12 = (bf16[2,320,160]{1,2,0:T(8,128)(2,1)S(1)}, bf16[2,320,160]{1,2,0:T(8,128)(2,1)S(1)}, u32[]{:S(2)}, u32[]{:S(2)}) collective-permute-start(bf16[2,320,160]{1,2,0:T(8,128)(2,1)S(1)} %collective-permute-done.10), channel_id=1, source_target_pairs={{0,1},{1,2},{2,3},{3,4},{4,5},{5,6},{6,7},{7,8},{8,9},{9,10},{10,1... | collective-permute-start | bytes 614408 | tf_op jit(solution)/shard_map/ppermute | solution.py:21
  103.3 8.5 %collective-permute-start.13 = (bf16[2,320,160]{1,2,0:T(8,128)(2,1)S(1)}, bf16[2,320,160]{1,2,0:T(8,128)(2,1)S(1)}, u32[]{:S(2)}, u32[]{:S(2)}) collective-permute-start(bf16[2,320,160]{1,2,0:T(8,128)(2,1)S(1)} %collective-permute-done.11), channel_id=1, source_target_pairs={{0,15},{1,0},{2,1},{3,2},{4,3},{5,4},{6,5},{7,6},{8,7},{9,8},{10,9... | collective-permute-start | bytes 614408 | tf_op jit(solution)/shard_map/ppermute | solution.py:26
  111.7 8.3 %collective-permute-start.14 = (bf16[2,320,160]{1,2,0:T(8,128)(2,1)S(1)}, bf16[2,320,160]{1,2,0:T(8,128)(2,1)S(1)}, u32[]{:S(2)}, u32[]{:S(2)}) collective-permute-start(bf16[2,320,160]{1,2,0:T(8,128)(2,1)S(1)} %collective-permute-done.12), channel_id=1, source_target_pairs={{0,1},{1,2},{2,3},{3,4},{4,5},{5,6},{6,7},{7,8},{8,9},{9,10},{10,1... | collective-permute-start | bytes 614408 | tf_op jit(solution)/shard_map/ppermute | solution.py:21
  120.1 1.9 %copy-start.1 = (bf16[2,320,2560]{1,2,0:T(8,128)(2,1)}, bf16[2,320,2560]{1,2,0:T(8,128)(2,1)S(1)}, u32[]{:S(2)}) copy-start(bf16[2,320,2560]{1,2,0:T(8,128)(2,1)S(1)} %constant_dynamic-update-slice_fusion.8) | copy-start | bytes 9830404
  122.9 6.0 %copy-start.2 = (bf16[2,320,2560]{1,2,0:T(8,128)(2,1)S(1)}, bf16[2,320,2560]{1,2,0:T(8,128)(2,1)}, u32[]{:S(2)}) copy-start(bf16[2,320,2560]{1,2,0:T(8,128)(2,1)} %copy-done.1) | copy-start | bytes 9830404
  127.7 2.5 %copy-start.5 = (bf16[1,2,32,320]{3,2,1,0:T(8,128)(2,1)S(1)}, bf16[1,2,32,320]{3,2,1,0:T(8,128)(2,1)}, u32[]{:S(2)}) copy-start(bf16[1,2,32,320]{3,2,1,0:T(8,128)(2,1)} %param.17) | copy-start | bytes 122884
  130.5 1.7 copy-start.7
  131.4 2.1 %copy-start.13 = (bf16[2,2560,16]{1,2,0:T(8,128)(2,1)S(1)}, bf16[2,2560,16]{1,2,0:T(8,128)(2,1)}, u32[]{:S(2)}) copy-start(bf16[2,2560,16]{1,2,0:T(8,128)(2,1)} %param.28) | copy-start | bytes 491524
  132.3 45.7 %copy-start.3 = (bf16[256,2048]{1,0:T(8,128)(2,1)S(1)}, bf16[256,2048]{1,0:T(8,128)(2,1)}, u32[]{:S(2)}) copy-start(bf16[256,2048]{1,0:T(8,128)(2,1)} %param.30) | copy-start | bytes 3145732
  132.3 45.7 %copy-start.12 = (f32[256]{0:T(256)S(1)}, f32[256]{0:T(256)}, u32[]{:S(2)}) copy-start(f32[256]{0:T(256)} %param.31) | copy-start | bytes 3076
Sparse Core Ops, SparseCore 0:
  12.3 41.8 all-gather.1
